TPU v7x, 32 devices: a whole 2x2x4 slice. The times are simulated.
32 devices in a mesh: groups: 2 (over x), events: 16 (over z, y, core).
Axes of the slice: x: 2, y: 2, z: 4, core: 2. Of those that a mesh axis runs over, the one named last changes fastest.
Arguments:
- waveforms: bfloat16 [64, 128, 1024], P(('groups', 'events')), parts along dimension 0, may hold values from -8 to 8
- matching: int32 [2, 32], P(None, 'groups'), parts along dimension 1, may hold values from 0 to 15, as said below
- available: int32 [64, 128, 2, 2], P(('groups', 'events')), parts along dimension 0, may hold values 0 or 1
Outputs:
- aligned_stack: bfloat16 [64, 128, 1024], P(('groups', 'events')), parts along dimension 0
- pair_scores: float32 [2, 64, 2, 128], P(None, ('groups', 'events')), parts along dimension 1
There are 2 independent parts, one for each index of `groups`. A program takes and returns all parts, laid end to end along the dimension named above; each array names one. Nothing has to cross between parts.
Inputs may be any that keep to these rules, and one draw needn't show every extreme that they name: `matching`: in each round a block's partner is another block, and the partner of its partner is the block itself.
All inputs are finite; a program needn't handle non-finite values. No bound on the sum of `available` on one device may be relied on, other than what follows from the above.
Results may differ from a plain program's by a relative error of at most 0.018.
Values may be sent and summed in bfloat16 or wider, within the bound.
A program may use at most 128 MiB of HBM per device.

v0:
```python
import math

import jax
import jax.numpy as jnp
from jax import lax
from jax.sharding import PartitionSpec as P

STATIONS = 128
SAMPLES = 1024
LAGS = 128
MLEN = 1152


def make_tables():
    times = jnp.arange(SAMPLES, dtype=jnp.int32)
    freqs = jnp.arange(MLEN, dtype=jnp.int32)
    lagset = (jnp.arange(LAGS, dtype=jnp.int32) - LAGS // 2) % MLEN
    angle_t = (times[:, None] * freqs[None, :] % MLEN).astype(jnp.float32) * (2.0 * math.pi / MLEN)
    angle_l = (freqs[:, None] * lagset[None, :] % MLEN).astype(jnp.float32) * (2.0 * math.pi / MLEN)
    forward = jnp.concatenate([jnp.cos(angle_t), -jnp.sin(angle_t)], axis=1).astype(jnp.bfloat16)
    corr_tab = (jnp.concatenate([jnp.cos(angle_l), -jnp.sin(angle_l)], axis=0) / MLEN).astype(
        jnp.bfloat16
    )
    spread_tab = jnp.concatenate([jnp.cos(angle_l).T, jnp.sin(angle_l).T], axis=1).astype(
        jnp.bfloat16
    )
    back_tab = (jnp.concatenate([jnp.cos(angle_t).T, -jnp.sin(angle_t).T], axis=0) / MLEN).astype(
        jnp.bfloat16
    )
    return (forward, corr_tab, spread_tab, back_tab)


def body(waveforms, matching, available):
    forward, corr_tab, spread_tab, back_tab = make_tables()
    blocksize = waveforms.shape[0]
    rounds = matching.shape[0]
    flags = available.astype(jnp.bfloat16)
    held, held_flags = (
        lax.all_to_all(waveforms, "events", split_axis=1, concat_axis=0, tiled=True),
        lax.all_to_all(flags, "events", split_axis=1, concat_axis=0, tiled=True),
    )
    count = held.shape[0]
    local = held.shape[1]
    spectra = jnp.dot(
        held.reshape(count * local, SAMPLES), forward, preferred_element_type=jnp.float32
    )
    spectra = spectra.astype(jnp.bfloat16).reshape(count, local, 2 * MLEN)
    blocks_of = jnp.repeat(matching, blocksize, axis=1)
    partner = (
        blocks_of[:, :, None] * blocksize + jnp.arange(blocksize, dtype=jnp.int32)[None, None, :]
    )
    other = spectra[partner].astype(jnp.float32)
    own = spectra[None, :, None].astype(jnp.float32)
    real_a, imag_a = (own[..., :MLEN], own[..., MLEN:])
    real_b, imag_b = (other[..., :MLEN], other[..., MLEN:])
    cross = jnp.concatenate(
        [real_a * real_b + imag_a * imag_b, real_a * imag_b - imag_a * real_b], axis=-1
    ).astype(jnp.bfloat16)
    corr = jnp.dot(cross.reshape(-1, 2 * MLEN), corr_tab, preferred_element_type=jnp.float32)
    corr = corr.reshape(rounds, count, blocksize, local, LAGS)
    weight_flags = jnp.transpose(held_flags, (2, 0, 3, 1)).astype(jnp.float32)
    partial_sum = jnp.sum(weight_flags[..., None] * corr, axis=3)
    scale = 2.0 / math.sqrt(SAMPLES * STATIONS)
    totals = lax.psum(partial_sum, "events")
    all_scores = totals * scale
    all_weights = jax.nn.softmax(all_scores, axis=-1).astype(jnp.bfloat16)
    scores = lax.dynamic_slice_in_dim(
        all_scores, lax.axis_index("events") * blocksize, blocksize, 1
    )
    spread = jnp.dot(all_weights.reshape(-1, LAGS), spread_tab, preferred_element_type=jnp.float32)
    spread = spread.reshape(rounds, count, blocksize, 1, 2 * MLEN)
    real_v, imag_v = (spread[..., :MLEN], spread[..., MLEN:])
    real_z = jnp.sum(real_v * real_b - imag_v * imag_b, axis=(0, 2))
    imag_z = jnp.sum(real_v * imag_b + imag_v * real_b, axis=(0, 2))
    zspec = jnp.concatenate([real_z, imag_z], axis=-1).astype(jnp.bfloat16)
    stacked = jnp.dot(zspec.reshape(-1, 2 * MLEN), back_tab, preferred_element_type=jnp.float32)
    stacked = stacked.reshape(count, local, SAMPLES).astype(jnp.bfloat16)
    returned = lax.all_to_all(stacked, "events", split_axis=0, concat_axis=1, tiled=True)
    return (returned, scores)


def solution(mesh):
    placed = (
        P(("groups", "events"), None, None),
        P(None, "groups"),
        P(("groups", "events"), None, None, None),
    )
    return jax.shard_map(
        body,
        mesh=mesh,
        in_specs=placed,
        out_specs=(P(("groups", "events"), None, None), P(None, ("groups", "events"), None, None)),
        check_vma=False,
    )
```

profile of v0, /device:TPU:15, one launch (start us, length us, event | category | flops | bytes accessed | tf_op | source)
XLA Modules:
  0.0 209.7 jit_solution(17493807019713771578)
XLA Ops:
  7.2 0.7 convert_element_type.83
  7.9 0.8 copy.32
  8.7 6.6 %all-to-all-start = ((bf16[2,128,2,2]{3,2,0,1:T(2,128)(2,1)}), bf16[2,128,2,2]{3,2,0,1:T(2,128)(2,1)S(1)}, u32[]{:S(2)}, u32[]{:S(2)}) async-start(bf16[2,128,2,2]{3,2,0,1:T(2,128)(2,1)} %copy.32), calls=%async_computation | async-start | bytes 262144 | tf_op jit(solution)/shard_map/all_to_all | solution.py:40
  15.3 20.4 %sine_negate_fusion = (f32[1152,1024]{1,0:T(8,128)}, f32[1152,1024]{1,0:T(8,128)}) fusion(), kind=kLoop, calls=%fused_computation.20 | loop fusion | flops 11796480 | bytes 9437184 | tf_op jit(solution)/shard_map/neg | solution.py:27
  36.1 1.3 copy.36
  37.4 6.0 %all-to-all-start.1 = ((bf16[2,128,1024]{2,0,1:T(2,128)(2,1)}), bf16[2,128,1024]{2,0,1:T(2,128)(2,1)S(1)}, u32[]{:S(2)}, u32[]{:S(2)}) async-start(bf16[2,128,1024]{2,0,1:T(2,128)(2,1)} %copy.36), calls=%async_computation.1 | async-start | bytes 1048576 | tf_op jit(solution)/shard_map/all_to_all | solution.py:39
  43.7 3.3 %fusion.55 = (f32[1152,128]{1,0:T(8,128)}, f32[1152,128]{1,0:T(8,128)}) fusion(s32[128]{0:T(128)S(1)} %and_select_fusion), kind=kLoop, calls=%fused_computation.73 | loop fusion | flops 1474560 | bytes 1180160 | tf_op jit(solution)/shard_map/cos | solution.py:21
  47.0 20.5 %negate_convert_fusion = (bf16[1024,1152]{1,0:T(8,128)(2,1)S(1)}, bf16[1024,1152]{1,0:T(8,128)(2,1)}) fusion(), kind=kLoop, calls=%fused_computation.29 | loop fusion | flops 14155776 | bytes 4718592 | tf_op jit(solution)/shard_map/convert.12
  67.8 0.7 copy.35
  68.7 4.5 %bitcast_convert_fusion = (f32[1,32,1,8,2304]{4,3,1,2,0:T(8,128)}, bf16[2304,256]{0,1:T(8,128)(2,1)S(1)}) fusion(bf16[256,1024]{1,0:T(8,128)(2,1)S(1)} %bitcast.65, bf16[1024,1152]{1,0:T(8,128)(2,1)S(1)} %get-tuple-element.18, bf16[1024,1152]{1,0:T(8,128)(2,1)} %get-tuple-element.19), kind=kOutput, calls=%fused_computation.47 | convolution fusion | flops 1218576384 | bytes 8781824 | tf_op jit(solution)/shard_map/dot_general | solution.py:44
  73.1 3.0 %gather_fusion = bf16[128,8,2304]{2,1,0:T(8,128)(2,1)} fusion(bf16[32,8,2304]{2,1,0:T(8,128)(2,1)S(1)} %bitcast.58, s32[1024]{0:T(1024)S(1)} %pad_clamp_fusion), kind=kCustom, calls=%fused_computation | custom fusion | bytes 9437696 | tf_op jit(solution)/shard_map/gather | solution.py:52
  76.1 3.7 %bitcast_convert_fusion.1 = f32[2,32,2,8,2304]{4,3,2,1,0:T(8,128)S(1)} fusion(bf16[128,8,2304]{2,1,0:T(8,128)(2,1)} %gather_fusion), kind=kLoop, calls=%fused_computation.92 | loop fusion | flops 2359296 | bytes 14155776 | tf_op jit(solution)/shard_map/convert_element_type | solution.py:52
  80.0 1.8 add_convert_fusion
  81.8 1.7 copy-done
  83.5 2.1 %fusion.37 = f32[2,32,2,128]{3,2,1,0:T(2,128)} fusion(bf16[2,32,2,8,1152]{4,3,2,1,0:T(8,128)(2,1)S(1)} %get-tuple-element.5, bf16[2,32,2,8,1152]{4,3,2,1,0:T(8,128)(2,1)S(1)} %get-tuple-element.4, f32[1152,128]{1,0:T(8,128)S(1)} %copy-done.3, f32[1152,128]{1,0:T(8,128)S(1)} %copy-done.2, f32[2,32,2,8]{3,2,1,0:T(2,128)S(1)} %copy-done.6), kind=kOutput, calls=%fused_computation.48 | convolution fusion | flops 614547456 | bytes 5967872 | tf_op jit(solution)/shard_map/dot_general | solution.py:59
  85.7 2.8 %cosine_convert_fusion.1 = (bf16[128,1152]{1,0:T(8,128)(2,1)S(1)}, bf16[128,1152]{1,0:T(8,128)(2,1)S(1)}) fusion(s32[128]{0:T(128)S(1)} %and_select_fusion), kind=kLoop, calls=%fused_computation.64 | loop fusion | flops 1622016 | bytes 590336 | tf_op jit(solution)/shard_map/convert.7
  88.5 81.1 %all-reduce.2.cloned.1.call-done = f32[2,32,2,128]{3,2,1,0:T(2,128)} async-done(((f32[2,32,2,128]{3,2,1,0:T(2,128)}), f32[2,32,2,128]{3,2,1,0:T(2,128)}) %all-reduce.2.cloned.1.call-update) | async-done | bytes 65552 | tf_op jit(solution)/shard_map/psum | solution.py:64
  169.6 1.1 fusion.68
  172.2 5.5 %subtract_reduce_fusion = (bf16[32,8,1152]{2,1,0:T(8,128)(2,1)S(1)}, bf16[32,8,1152]{2,1,0:T(8,128)(2,1)S(1)}) fusion(f32[2,32,2,8,2304]{4,3,2,1,0:T(8,128)} %copy-done, f32[2,32,2,1152]{3,2,1,0:T(2,128)S(1)} %copy.41, f32[2,32,2,1152]{3,2,1,0:T(2,128)S(1)} %copy.40), kind=kLoop, calls=%fused_computation.26 | loop fusion | flops 8847360 | bytes 11796480 | tf_op jit(solution)/shard_map/reduce_sum | solution.py:73
  177.8 2.3 %fusion.27 = bf16[32,8,1024]{2,1,0:T(8,128)(2,1)} fusion(f32[1152,1024]{1,0:T(8,128)S(1)} %bitcast.60, f32[1152,1024]{1,0:T(8,128)S(1)} %bitcast.62, bf16[32,8,1152]{2,1,0:T(8,128)(2,1)S(1)} %get-tuple-element.3, bf16[32,8,1152]{2,1,0:T(8,128)(2,1)S(1)} %get-tuple-element.2), kind=kOutput, calls=%fused_computation.38 | convolution fusion | flops 1217658880 | bytes 11141120 | tf_op jit(solution)/shard_map/dot_general | solution.py:76
  180.1 8.3 %all-to-all-start.2 = ((bf16[32,8,1024]{2,1,0:T(8,128)(2,1)}), bf16[32,8,1024]{2,1,0:T(8,128)(2,1)S(1)}, u32[]{:S(2)}, u32[]{:S(2)}) async-start(bf16[32,8,1024]{2,1,0:T(8,128)(2,1)} %fusion.27), calls=%async_computation.2 | async-start | bytes 1048576 | tf_op jit(solution)/shard_map/all_to_all | solution.py:78
  188.5 0.6 constant_dynamic-slice_fusion
  189.1 12.9 %all-to-all-done.2 = bf16[32,8,1024]{2,1,0:T(8,128)(2,1)S(1)} async-done(((bf16[32,8,1024]{2,1,0:T(8,128)(2,1)}), bf16[32,8,1024]{2,1,0:T(8,128)(2,1)S(1)}, u32[]{:S(2)}, u32[]{:S(2)}) %all-to-all-start.2) | async-done | bytes 524320 | tf_op jit(solution)/shard_map/all_to_all | solution.py:78
  202.0 0.8 copy.49
  (48 shorter events, 2.9 us)
Async XLA Ops:
  8.7 28.7 %all-to-all-start = ((bf16[2,128,2,2]{3,2,0,1:T(2,128)(2,1)}), bf16[2,128,2,2]{3,2,0,1:T(2,128)(2,1)S(1)}, u32[]{:S(2)}, u32[]{:S(2)}) async-start(bf16[2,128,2,2]{3,2,0,1:T(2,128)(2,1)} %copy.32), calls=%async_computation | async-start | bytes 262144 | tf_op jit(solution)/shard_map/all_to_all | solution.py:40
  15.2 20.4 %copy-start.7 = (s32[2,16]{1,0:T(2,128)S(1)}, s32[2,16]{1,0:T(2,128)}, u32[]{:S(2)}) copy-start(s32[2,16]{1,0:T(2,128)} %param.4) | copy-start | bytes 388
  15.3 20.8 %copy-start.4 = (bf16[2,128,1024]{2,1,0:T(8,128)(2,1)S(1)}, bf16[2,128,1024]{2,1,0:T(8,128)(2,1)}, u32[]{:S(2)}) copy-start(bf16[2,128,1024]{2,1,0:T(8,128)(2,1)} %param.3) | copy-start | bytes 1572868
  37.4 31.1 %all-to-all-start.1 = ((bf16[2,128,1024]{2,0,1:T(2,128)(2,1)}), bf16[2,128,1024]{2,0,1:T(2,128)(2,1)S(1)}, u32[]{:S(2)}, u32[]{:S(2)}) async-start(bf16[2,128,1024]{2,0,1:T(2,128)(2,1)} %copy.36), calls=%async_computation.1 | async-start | bytes 1048576 | tf_op jit(solution)/shard_map/all_to_all | solution.py:39
  43.4 126.1 %all-reduce.2.cloned.1.call-start = ((), (), s32[]{:S(2)}) async-start(), calls=%async_computation.3 | async-start | bytes 131072 | tf_op jit(solution)/shard_map/psum | solution.py:64
  76.1 3.8 %copy-start.1 = (f32[1,32,1,8,2304]{4,3,1,2,0:T(8,128)S(1)}, f32[1,32,1,8,2304]{4,3,1,2,0:T(8,128)}, u32[]{:S(2)}) copy-start(f32[1,32,1,8,2304]{4,3,1,2,0:T(8,128)} %get-tuple-element.14) | copy-start | bytes 7077892
  79.8 3.7 %copy-start = (f32[2,32,2,8,2304]{4,3,2,1,0:T(8,128)}, f32[2,32,2,8,2304]{4,3,2,1,0:T(8,128)S(1)}, u32[]{:S(2)}) copy-start(f32[2,32,2,8,2304]{4,3,2,1,0:T(8,128)S(1)} %bitcast_convert_fusion.1) | copy-start | bytes 28311556
  80.0 3.5 %copy-start.2 = (f32[1152,128]{1,0:T(8,128)S(1)}, f32[1152,128]{1,0:T(8,128)}, u32[]{:S(2)}) copy-start(f32[1152,128]{1,0:T(8,128)} %get-tuple-element.10) | copy-start | bytes 1769476
  80.0 3.5 %copy-start.3 = (f32[1152,128]{1,0:T(8,128)S(1)}, f32[1152,128]{1,0:T(8,128)}, u32[]{:S(2)}) copy-start(f32[1152,128]{1,0:T(8,128)} %get-tuple-element.11) | copy-start | bytes 1769476
  80.0 3.5 %copy-start.6 = (f32[2,32,2,8]{3,2,1,0:T(2,128)S(1)}, f32[2,32,2,8]{3,2,1,0:T(2,128)}, u32[]{:S(2)}) copy-start(f32[2,32,2,8]{3,2,1,0:T(2,128)} %copy.35) | copy-start | bytes 12292
  171.2 6.5 %slice-start.2 = ((s8[4718592]{0:T(1024)(128)(4,1)}), s8[4194304]{0:T(1024)(128)(4,1)S(1)}, s32[]{:S(2)}) async-start(s8[4718592]{0:T(1024)(128)(4,1)} %bitcast.61), calls=%async_computation.6 | async-start | bytes 8388608
  171.7 6.0 %slice-start = ((s8[4718592]{0:T(1024)(128)(4,1)}), s8[4194304]{0:T(1024)(128)(4,1)S(1)}, s32[]{:S(2)}) async-start(s8[4718592]{0:T(1024)(128)(4,1)} %bitcast.59), calls=%async_computation.4 | async-start | bytes 8388608
  172.1 5.5 %slice-start.1 = ((s8[4718592]{0:T(1024)(128)(4,1)}), s8[524288]{0:T(1024)(128)(4,1)S(1)}, s32[]{:S(2)}) async-start(s8[4718592]{0:T(1024)(128)(4,1)} %bitcast.59), calls=%async_computation.5 | async-start | bytes 1048576
  172.1 5.7 %slice-start.3 = ((s8[4718592]{0:T(1024)(128)(4,1)}), s8[524288]{0:T(1024)(128)(4,1)S(1)}, s32[]{:S(2)}) async-start(s8[4718592]{0:T(1024)(128)(4,1)} %bitcast.61), calls=%async_computation.7 | async-start | bytes 1048576
  177.8 10.6 %copy-start.5 = (f32[2,32,2,128]{3,2,1,0:T(2,128)S(1)}, f32[2,32,2,128]{3,2,1,0:T(2,128)}, u32[]{:S(2)}) copy-start(f32[2,32,2,128]{3,2,1,0:T(2,128)} %all-reduce.2.cloned.1.call-done) | copy-start | bytes 196612
  180.1 21.9 %all-to-all-start.2 = ((bf16[32,8,1024]{2,1,0:T(8,128)(2,1)}), bf16[32,8,1024]{2,1,0:T(8,128)(2,1)S(1)}, u32[]{:S(2)}, u32[]{:S(2)}) async-start(bf16[32,8,1024]{2,1,0:T(8,128)(2,1)} %fusion.27), calls=%async_computation.2 | async-start | bytes 1048576 | tf_op jit(solution)/shard_map/all_to_all | solution.py:78
Sparse Core Ops, SparseCore 0:
  85.8 83.7 all-reduce.1
where the time goes:
time: 212 us; the launch traced here: 210 us
  waiting for transfers between devices  94.1 us (44%)
  other arithmetic  60.1 us (28%)
  starting transfers between devices  21.1 us (10%)
  between operations  14.3 us (7%)
  local copies, waits for them, and re-layouts  11 us (5%)
  matrix products  9.16 us (4%)
    psum x1, waiting for transfers between devices, body(): totals = lax.psum(partial_sum, 'events')  81.1 us
    another operation x3, other arithmetic  25.1 us
    neg x1, other arithmetic, make_tables(): -jnp.sin(angle_t).T  20.4 us
    all_to_all x1, waiting for transfers between devices, body(): lax.all_to_all(stacked, 'events', split_axis=0, concat_axis=1, tiled=True)  12.9 us
    all_to_all x1, starting transfers between devices, body(): lax.all_to_all(stacked, 'events', split_axis=0, concat_axis=1, tiled=True)  8.32 us
    all_to_all x1, starting transfers between devices, body(): lax.all_to_all(flags, 'events', split_axis=1, concat_axis=0, tiled=True)  6.55 us
    all_to_all x1, starting transfers between devices, body(): lax.all_to_all(waveforms, 'events', split_axis=1, concat_axis=0, tiled=True)  6.02 us
    reduce_sum x1, other arithmetic, body(): real_z = jnp.sum(real_v * real_b - imag_v * imag_b, axis=(0, 2))  5.48 us
  transfers between devices with their start and end apart: 4, of which 2 were waited for; matrix products, arithmetic and copies ran while one was open for 24% of the time, Pallas kernels for 0%

commit v1 on v0

v1 whole, which is shorter than its diff:
```python
import functools
import math

import jax
import jax.numpy as jnp
import ml_dtypes
import numpy as np
from jax import lax
from jax.experimental import pallas as pl
from jax.experimental.pallas import tpu as pltpu
from jax.sharding import PartitionSpec as P

LAGS = 128
LANES = 128
MESH = pl.DeviceIdType.MESH


def transform_length(samples):
    return samples + LAGS


def make_tables(samples):
    mlen = transform_length(samples)
    times = np.arange(samples, dtype=np.int64)
    freqs = np.arange(mlen, dtype=np.int64)
    lagset = (np.arange(LAGS, dtype=np.int64) - LAGS // 2) % mlen
    step = np.float32(2.0 * math.pi / mlen)
    angle_t = (times[:, None] * freqs[None, :] % mlen).astype(np.float32) * step
    angle_l = (freqs[:, None] * lagset[None, :] % mlen).astype(np.float32) * step
    return mlen, (np.cos(angle_t), np.sin(angle_t)), (np.cos(angle_l), np.sin(angle_l))


def full_tables(samples):
    mlen, (ct, st), (cl, sl) = make_tables(samples)
    bf = ml_dtypes.bfloat16
    return (
        np.concatenate([ct, -st], axis=1).astype(bf),
        (np.concatenate([cl, -sl], axis=0) / np.float32(mlen)).astype(bf),
        np.concatenate([cl.T, sl.T], axis=1).astype(bf),
        (np.concatenate([ct.T, -st.T], axis=0) / np.float32(mlen)).astype(bf),
    )


def half_tables(samples):
    mlen, (ct, st), (cl, sl) = make_tables(samples)
    bf = ml_dtypes.bfloat16
    bins = mlen // 2 + 1
    padded = -(-bins // LANES) * LANES
    twice = np.full((bins, 1), 2.0, np.float32)
    twice[0] = 1.0
    if mlen % 2 == 0:
        twice[-1] = 1.0

    def cols(x):
        return np.pad(x[:, :bins], ((0, 0), (0, padded - bins)))

    def rows(x):
        return np.pad(x[:bins] * twice / np.float32(mlen), ((0, padded - bins), (0, 0)))

    return padded, (
        np.concatenate([cols(ct), cols(-st)], axis=1).astype(bf),
        np.concatenate([rows(cl), rows(-sl)], axis=0).astype(bf),
        np.concatenate([cols(cl.T), cols(sl.T)], axis=1).astype(bf),
        np.concatenate([rows(ct.T), rows(-st.T)], axis=0).astype(bf),
    )


def kernel(
    n, eb, rounds, local, samples, bins, group, scale,
    match_ref, wave_ref, fwd_hbm, ctab_hbm, stab_hbm, back_hbm,
    out_ref, scores_ref,
    recv, fwd, ctab, stab, back, spec, cross, mask, part, score_in, wts, spread, zspec, sendb,
    tab_sem, own_sem, s1, r1, s2, r2, s3, r3, s4, r4,
):
    me = lax.axis_index("events")
    rows = eb * local
    pairs = rounds * eb * eb

    def ahead(k):
        return lax.rem(me + k, n)

    def behind(k):
        return lax.rem(me + n - k, n)

    tables = [
        pltpu.make_async_copy(src, dst, tab_sem.at[i])
        for i, (src, dst) in enumerate(
            ((fwd_hbm, fwd), (ctab_hbm, ctab), (stab_hbm, stab), (back_hbm, back))
        )
    ]
    own_in = pltpu.make_async_copy(wave_ref.at[me], recv.at[0], own_sem.at[0])
    own_in.start()
    for table in tables:
        table.start()

    barrier = pltpu.get_barrier_semaphore()

    @pl.loop(1, n)
    def _(k):
        pl.semaphore_signal(barrier, inc=1, device_id={"events": ahead(k)}, device_id_type=MESH)

    pl.semaphore_wait(barrier, n - 1)

    def wave_copy(k):
        return pltpu.make_async_remote_copy(
            src_ref=wave_ref.at[ahead(k)], dst_ref=recv.at[k], send_sem=s1.at[k],
            recv_sem=r1.at[k], device_id={"events": ahead(k)}, device_id_type=MESH,
        )

    def part_copy(k):
        return pltpu.make_async_remote_copy(
            src_ref=part.at[k], dst_ref=score_in.at[k], send_sem=s2.at[k],
            recv_sem=r2.at[k], device_id={"events": behind(k)}, device_id_type=MESH,
        )

    def weight_copy(k):
        return pltpu.make_async_remote_copy(
            src_ref=wts.at[0], dst_ref=wts.at[k], send_sem=s3.at[k],
            recv_sem=r3.at[k], device_id={"events": ahead(k)}, device_id_type=MESH,
        )

    def stack_copy(k):
        return pltpu.make_async_remote_copy(
            src_ref=sendb.at[k], dst_ref=out_ref.at[me], send_sem=s4.at[k],
            recv_sem=r4.at[k], device_id={"events": behind(k)}, device_id_type=MESH,
        )

    @pl.loop(1, n)
    def _(k):
        wave_copy(k).start()

    own_in.wait()
    tables[0].wait()

    def spectra(first):
        wave = recv[pl.ds(first, group), :, :samples].reshape(group * rows, samples)
        got = jnp.dot(wave, fwd[...], preferred_element_type=jnp.float32)
        spec[pl.ds(first * eb, group * eb)] = got.reshape(group * eb, local, 2 * bins)

    @pl.loop(0, n // group)
    def _(g):
        @pl.loop(0, group)
        def _(i):
            @pl.when(g * group + i > 0)
            def _():
                wave_copy(g * group + i).wait_recv()

        spectra(g * group)

    def partner_slot(r, c):
        return lax.rem(me + n - match_ref[r, behind(c)], n)

    @pl.loop(0, n)
    def _(c):
        flags = recv[c, :, samples:].astype(jnp.float32)
        for r in range(rounds):
            p = partner_slot(r, c)
            for e in range(eb):
                ar = spec[c * eb + e, :, :bins]
                ai = spec[c * eb + e, :, bins:]
                real, imag = [], []
                for j in range(eb):
                    br = spec[p * eb + j, :, :bins]
                    bi = spec[p * eb + j, :, bins:]
                    real.append(ar * br + ai * bi)
                    imag.append(ar * bi - ai * br)
                    lane = r * eb + j
                    flag = flags[e * local:(e + 1) * local, lane:lane + 1]
                    mask[c * pairs + (r * eb + e) * eb + j] = jnp.broadcast_to(flag, (local, LAGS))
                at = (c * rounds + r) * eb + e
                cross[at, :, :bins] = jnp.concatenate(real, axis=0).astype(jnp.bfloat16)
                cross[at, :, bins:] = jnp.concatenate(imag, axis=0).astype(jnp.bfloat16)

    tables[1].wait()

    @pl.loop(0, n // group)
    def _(g):
        block = cross[pl.ds(g * group * rounds * eb, group * rounds * eb)]
        corr = jnp.dot(
            block.reshape(group * pairs * local, 2 * bins), ctab[...],
            preferred_element_type=jnp.float32,
        ).reshape(group * pairs, local, LAGS)
        total = jnp.sum(corr * mask[pl.ds(g * group * pairs, group * pairs)], axis=1)
        part[pl.ds(g * group, group)] = total.reshape(group, pairs, LAGS)

    @pl.loop(1, n)
    def _(k):
        part_copy(k).start()

    @pl.loop(1, n)
    def _(k):
        part_copy(k).wait_recv()

    total = part[0]
    for k in range(1, n):
        total = total + score_in[k]
    scores = total * scale
    scores_ref[...] = scores
    grown = jnp.exp(scores - jnp.max(scores, axis=-1, keepdims=True))
    wts[0] = grown / jnp.sum(grown, axis=-1, keepdims=True)

    @pl.loop(1, n)
    def _(k):
        weight_copy(k).start()

    tables[2].wait()
    tables[3].wait()

    @pl.loop(1, n)
    def _(k):
        weight_copy(k).wait_recv()

    spread[...] = jnp.dot(
        wts[...].reshape(n * pairs, LAGS).astype(jnp.bfloat16), stab[...],
        preferred_element_type=jnp.float32,
    ).reshape(n, pairs, 2 * bins)

    @pl.loop(0, n // group)
    def _(g):
        @pl.loop(0, group)
        def _(i):
            c = g * group + i
            real = [None] * eb
            imag = [None] * eb
            for r in range(rounds):
                p = partner_slot(r, c)
                for j in range(eb):
                    yr = spec[p * eb + j, :, :bins]
                    yi = spec[p * eb + j, :, bins:]
                    for e in range(eb):
                        at = (r * eb + e) * eb + j
                        vr = spread[c, at:at + 1, :bins]
                        vi = spread[c, at:at + 1, bins:]
                        zr = vr * yr - vi * yi
                        zi = vr * yi + vi * yr
                        real[e] = zr if real[e] is None else real[e] + zr
                        imag[e] = zi if imag[e] is None else imag[e] + zi
            zspec[c, :, :bins] = jnp.concatenate(real, axis=0).astype(jnp.bfloat16)
            zspec[c, :, bins:] = jnp.concatenate(imag, axis=0).astype(jnp.bfloat16)

        got = jnp.dot(
            zspec[pl.ds(g * group, group)].reshape(group * rows, 2 * bins), back[...],
            preferred_element_type=jnp.float32,
        )
        sendb[pl.ds(g * group, group)] = got.astype(jnp.bfloat16).reshape(group, rows, samples)

        @pl.loop(0, group)
        def _(i):
            @pl.when(g * group + i > 0)
            def _():
                stack_copy(g * group + i).start()

    own_out = pltpu.make_async_copy(sendb.at[0], out_ref.at[me], own_sem.at[1])
    own_out.start()

    @pl.loop(1, n)
    def _(k):
        wave_copy(k).wait_send()
        part_copy(k).wait_send()
        weight_copy(k).wait_send()
        stack_copy(k).wait_send()
        stack_copy(k).wait_recv()

    own_out.wait()


def kernel_body(n, waveforms, matching, available):
    eb, stations, samples = waveforms.shape
    rounds = matching.shape[0]
    local = stations // n
    rows = eb * local
    pairs = rounds * eb * eb
    bins, tables = half_tables(samples)
    group = 4 if n % 4 == 0 else 1
    flags = available.astype(jnp.bfloat16).reshape(eb, stations, rounds * eb)
    flags = jnp.pad(flags, ((0, 0), (0, 0), (0, LANES - rounds * eb)))
    packed = jnp.concatenate([waveforms, flags], axis=-1)
    wide = samples + LANES
    packed = packed.reshape(eb, n, local, wide).transpose(1, 0, 2, 3).reshape(n, rows, wide)
    bf, f32 = jnp.bfloat16, jnp.float32
    vmem, dma = pltpu.VMEM, pltpu.SemaphoreType.DMA
    anywhere = pl.BlockSpec(memory_space=pl.ANY)
    stacks, scores = pl.pallas_call(
        functools.partial(
            kernel, n, eb, rounds, local, samples, bins, group,
            2.0 / math.sqrt(samples * stations),
        ),
        out_shape=(
            jax.ShapeDtypeStruct((n, rows, samples), bf),
            jax.ShapeDtypeStruct((pairs, LAGS), f32),
        ),
        in_specs=[pl.BlockSpec(memory_space=pltpu.SMEM)] + [anywhere] * 5,
        out_specs=(anywhere, pl.BlockSpec(memory_space=pltpu.VMEM)),
        scratch_shapes=[
            vmem((n, rows, wide), bf),
            vmem(tables[0].shape, bf),
            vmem(tables[1].shape, bf),
            vmem(tables[2].shape, bf),
            vmem(tables[3].shape, bf),
            vmem((n * eb, local, 2 * bins), f32),
            vmem((n * rounds * eb, rows, 2 * bins), bf),
            vmem((n * pairs, local, LAGS), f32),
            vmem((n, pairs, LAGS), f32),
            vmem((n, pairs, LAGS), f32),
            vmem((n, pairs, LAGS), f32),
            vmem((n, pairs, 2 * bins), f32),
            vmem((n, rows, 2 * bins), bf),
            vmem((n, rows, samples), bf),
            dma((4,)),
            dma((2,)),
        ] + [dma((n,))] * 8,
        compiler_params=pltpu.CompilerParams(
            collective_id=0, has_side_effects=True, vmem_limit_bytes=56 * 1024 * 1024
        ),
    )(matching, packed, *(jnp.asarray(t) for t in tables))
    stacks = stacks.reshape(n, eb, local, samples).transpose(1, 0, 2, 3)
    return stacks.reshape(eb, stations, samples), scores.reshape(rounds, eb, eb, LAGS)


def plain_body(waveforms, matching, available):
    eb, stations, samples = waveforms.shape
    mlen = transform_length(samples)
    forward, corr_tab, spread_tab, back_tab = (jnp.asarray(t) for t in full_tables(samples))
    rounds = matching.shape[0]
    flags = available.astype(jnp.bfloat16)
    held = lax.all_to_all(waveforms, "events", split_axis=1, concat_axis=0, tiled=True)
    held_flags = lax.all_to_all(flags, "events", split_axis=1, concat_axis=0, tiled=True)
    count, local = held.shape[:2]
    blocks = count // eb
    spectra = jnp.dot(
        held.reshape(count * local, samples), forward, preferred_element_type=jnp.float32
    )
    spectra = spectra.astype(jnp.bfloat16).reshape(count, local, 2 * mlen)
    chosen = (matching[:, :, None] == jnp.arange(blocks)[None, None, :]).astype(jnp.bfloat16)
    other = jnp.dot(
        chosen.reshape(rounds * blocks, blocks), spectra.reshape(blocks, eb * local * 2 * mlen),
        preferred_element_type=jnp.float32,
    ).reshape(rounds, blocks, 1, eb, local, 2 * mlen)
    own = spectra.reshape(1, blocks, eb, 1, local, 2 * mlen).astype(jnp.float32)
    real_a, imag_a = (own[..., :mlen], own[..., mlen:])
    real_b, imag_b = (other[..., :mlen], other[..., mlen:])
    cross = jnp.concatenate(
        [real_a * real_b + imag_a * imag_b, real_a * imag_b - imag_a * real_b], axis=-1
    ).astype(jnp.bfloat16)
    corr = jnp.dot(cross.reshape(-1, 2 * mlen), corr_tab, preferred_element_type=jnp.float32)
    corr = corr.reshape(rounds, count, eb, local, LAGS)
    weight_flags = jnp.transpose(held_flags, (2, 0, 3, 1)).astype(jnp.float32)
    totals = lax.psum(jnp.sum(weight_flags[..., None] * corr, axis=3), "events")
    all_scores = totals * (2.0 / math.sqrt(samples * stations))
    all_weights = jax.nn.softmax(all_scores, axis=-1).astype(jnp.bfloat16)
    scores = lax.dynamic_slice_in_dim(all_scores, lax.axis_index("events") * eb, eb, 1)
    spread = jnp.dot(all_weights.reshape(-1, LAGS), spread_tab, preferred_element_type=jnp.float32)
    spread = spread.reshape(rounds, blocks, eb, eb, 1, 2 * mlen)
    real_v, imag_v = (spread[..., :mlen], spread[..., mlen:])
    real_z = jnp.sum(real_v * real_b - imag_v * imag_b, axis=(0, 3))
    imag_z = jnp.sum(real_v * imag_b + imag_v * real_b, axis=(0, 3))
    zspec = jnp.concatenate([real_z, imag_z], axis=-1).astype(jnp.bfloat16)
    stacked = jnp.dot(zspec.reshape(-1, 2 * mlen), back_tab, preferred_element_type=jnp.float32)
    stacked = stacked.reshape(count, local, samples).astype(jnp.bfloat16)
    returned = lax.all_to_all(stacked, "events", split_axis=0, concat_axis=1, tiled=True)
    return (returned, scores)


def solution(mesh):
    n = mesh.shape["events"]
    placed = (
        P(("groups", "events"), None, None),
        P(None, "groups"),
        P(("groups", "events"), None, None, None),
    )

    def body(waveforms, matching, available):
        eb, stations, _ = waveforms.shape
        if stations % n == 0 and (stations // n) % 8 == 0 and eb * (stations // n) % 16 == 0:
            return kernel_body(n, waveforms, matching, available)
        return plain_body(waveforms, matching, available)

    return jax.shard_map(
        body,
        mesh=mesh,
        in_specs=placed,
        out_specs=(P(("groups", "events"), None, None), P(None, ("groups", "events"), None, None)),
        check_vma=False,
    )
```

time: 212 us -> 58.5 us (0.28)
  the two profiles are of different devices: /device:TPU:15 before, /device:TPU:0 now
where the time goes in v1:
time: 58.5 us; the launch traced here: 58.2 us
  Pallas kernels  51.7 us (88%)
  local copies, waits for them, and re-layouts  3.3 us (6%)
  other arithmetic  2.59 us (4%)
  between operations  0.64 us (1%)
    pallas_call x1, Pallas kernels, kernel_body(): pl.pallas_call(functools.partial(kernel, n, eb, rounds, local, samples, b...  51.7 us
    reshape x1, other arithmetic, kernel_body(): packed.reshape(eb, n, local, wide).transpose(1, 0, 2, 3)  1.9 us
    reshape x1, local copies, waits for them, and re-layouts, kernel_body(): stacks.reshape(eb, stations, samples)  1.87 us
    unnamed x1, local copies, waits for them, and re-layouts  1.28 us

profile of v1, /device:TPU:0, one launch (start us, length us, event | category | flops | bytes accessed | tf_op | source)
XLA Modules:
  0.0 58.2 jit_solution(9300134406159297673)
XLA Ops:
  0.6 0.7 %convert_element_type.5 = bf16[2,128,2,2]{1,3,2,0:T(2,128)(2,1)S(1)} convert(s32[2,128,2,2]{1,3,2,0:T(2,128)} %param.9) | non-fusion elementwise | flops 1024 | bytes 6144 | tf_op jit(solution)/shard_map/convert_element_type | solution.py:275
  1.3 0.1 copy.9
  1.5 1.9 %copy_bitcast_fusion.wave_ref = bf16[16,16,1152]{2,1,0:T(8,128)(2,1)} fusion(bf16[2,128,4]{2,1,0:T(8,128)(2,1)S(1)} %copy.9, bf16[2,128,1024]{2,1,0:T(8,128)(2,1)} %param.7), kind=kLoop, calls=%fused_computation.4 | loop fusion | flops 1769472 | bytes 1116160 | tf_op jit(solution)/shard_map/reshape | solution.py:279
  3.4 51.7 %shard_map.86 = (bf16[16,16,1024]{2,1,0:T(8,128)(2,1)}, f32[8,128]{1,0:T(8,128)}) custom-call(s32[2,16]{1,0:T(2,128)} %match_ref.1, bf16[16,16,1152]{2,1,0:T(8,128)(2,1)} %copy_bitcast_fusion.wave_ref, bf16[1024,1280]{1,0:T(8,128)(2,1)} %constant.11.clone.fwd_hbm, bf16[1280,128]{1,0:T(8,128)(2,1)} %constant.12.clone.ctab_hbm, ...), custom_call_target="tpu_custom_call" | custom-call | tf_op jit(solution)/shard_map/pallas_call | solution.py:283
  55.1 1.9 %copy_bitcast_fusion.1 = bf16[2,128,1024]{2,1,0:T(8,128)(2,1)} fusion(bf16[16,16,1024]{2,1,0:T(8,128)(2,1)} %get-tuple-element.4), kind=kLoop, calls=%fused_computation.5 | loop fusion | bytes 1048576 | tf_op jit(solution)/shard_map/reshape | solution.py:317
  56.9 1.3 %copy.15 = f32[2,2,2,128]{3,2,1,0:T(2,128)} copy(f32[2,2,2,128]{3,2,1,0:T(2,128)} %bitcast.17) | data formatting | bytes 8192

commit v2 on v1

--- a/solution.py
+++ b/solution.py
@@ -66,10 +66,10 @@
 
 
 def kernel(
-    n, eb, rounds, local, samples, bins, group, scale,
-    match_ref, wave_ref, fwd_hbm, ctab_hbm, stab_hbm, back_hbm,
+    n, eb, rounds, local, stations, samples, bins, group, scale,
+    match_ref, flag_ref, wave_hbm, fwd_hbm, ctab_hbm, stab_hbm, back_hbm,
     out_ref, scores_ref,
-    recv, fwd, ctab, stab, back, spec, cross, mask, part, score_in, wts, spread, zspec, sendb,
+    wave, packed, recv, fwd, ctab, stab, back, spec, cross, part, score_in, wts, spread, zspec, sendb,
     tab_sem, own_sem, s1, r1, s2, r2, s3, r3, s4, r4,
 ):
     me = lax.axis_index("events")
@@ -88,7 +88,7 @@
             ((fwd_hbm, fwd), (ctab_hbm, ctab), (stab_hbm, stab), (back_hbm, back))
         )
     ]
-    own_in = pltpu.make_async_copy(wave_ref.at[me], recv.at[0], own_sem.at[0])
+    own_in = pltpu.make_async_copy(wave_hbm, wave, own_sem.at[0])
     own_in.start()
     for table in tables:
         table.start()
@@ -99,11 +99,31 @@
     def _(k):
         pl.semaphore_signal(barrier, inc=1, device_id={"events": ahead(k)}, device_id_type=MESH)
 
+    flags = jnp.concatenate(
+        [flag_ref[e, r] for r in range(rounds) for e in range(eb)], axis=0
+    ).astype(jnp.float32)
+    flags = jnp.concatenate(
+        [flags, jnp.zeros((rows - pairs, stations), jnp.float32)], axis=0
+    ).astype(jnp.bfloat16)
+    own_in.wait()
+
+    @pl.loop(0, n // 2)
+    def _(q):
+        traces = [
+            wave[e, pl.ds(pl.multiple_of(q * 2 * local, 2 * local), 2 * local), :].astype(jnp.float32)
+            for e in range(eb)
+        ]
+        for h in range(2):
+            packed[2 * q + h, :, :samples] = jnp.concatenate(
+                [t[h * local:(h + 1) * local] for t in traces], axis=0
+            ).astype(jnp.bfloat16)
+            packed[2 * q + h, :, samples:] = flags
+
     pl.semaphore_wait(barrier, n - 1)
 
     def wave_copy(k):
         return pltpu.make_async_remote_copy(
-            src_ref=wave_ref.at[ahead(k)], dst_ref=recv.at[k], send_sem=s1.at[k],
+            src_ref=packed.at[ahead(k)], dst_ref=recv.at[k], send_sem=s1.at[k],
             recv_sem=r1.at[k], device_id={"events": ahead(k)}, device_id_type=MESH,
         )
 
@@ -129,7 +149,7 @@
     def _(k):
         wave_copy(k).start()
 
-    own_in.wait()
+    recv[0] = packed[me]
     tables[0].wait()
 
     def spectra(first):
@@ -152,7 +172,6 @@
 
     @pl.loop(0, n)
     def _(c):
-        flags = recv[c, :, samples:].astype(jnp.float32)
         for r in range(rounds):
             p = partner_slot(r, c)
             for e in range(eb):
@@ -164,14 +183,15 @@
                     bi = spec[p * eb + j, :, bins:]
                     real.append(ar * br + ai * bi)
                     imag.append(ar * bi - ai * br)
-                    lane = r * eb + j
-                    flag = flags[e * local:(e + 1) * local, lane:lane + 1]
-                    mask[c * pairs + (r * eb + e) * eb + j] = jnp.broadcast_to(flag, (local, LAGS))
                 at = (c * rounds + r) * eb + e
                 cross[at, :, :bins] = jnp.concatenate(real, axis=0).astype(jnp.bfloat16)
                 cross[at, :, bins:] = jnp.concatenate(imag, axis=0).astype(jnp.bfloat16)
 
     tables[1].wait()
+    station = lax.broadcasted_iota(jnp.int32, (local, stations), 1)
+    first = me * local + lax.broadcasted_iota(jnp.int32, (local, stations), 0)
+    pick = jnp.where(station == first, 1.0, 0.0).astype(jnp.float32)
+    ones = jnp.ones((stations, LAGS), jnp.bfloat16)
 
     @pl.loop(0, n // group)
     def _(g):
@@ -180,7 +200,13 @@
             block.reshape(group * pairs * local, 2 * bins), ctab[...],
             preferred_element_type=jnp.float32,
         ).reshape(group * pairs, local, LAGS)
-        total = jnp.sum(corr * mask[pl.ds(g * group * pairs, group * pairs)], axis=1)
+        held = recv[pl.ds(g * group, group), :, samples:].astype(jnp.float32)[:, :pairs]
+        held = held.reshape(group * pairs, 1, stations) * pick[None]
+        mask = jnp.dot(
+            held.reshape(group * pairs * local, stations).astype(jnp.bfloat16), ones,
+            preferred_element_type=jnp.float32,
+        ).reshape(group * pairs, local, LAGS)
+        total = jnp.sum(corr * mask, axis=1)
         part[pl.ds(g * group, group)] = total.reshape(group, pairs, LAGS)
 
     @pl.loop(1, n)
@@ -195,7 +221,10 @@
     for k in range(1, n):
         total = total + score_in[k]
     scores = total * scale
-    scores_ref[...] = scores
+    for r in range(rounds):
+        for e in range(eb):
+            at = (r * eb + e) * eb
+            scores_ref[r, e] = scores[at:at + eb]
     grown = jnp.exp(scores - jnp.max(scores, axis=-1, keepdims=True))
     wts[0] = grown / jnp.sum(grown, axis=-1, keepdims=True)
 
@@ -216,7 +245,9 @@
     ).reshape(n, pairs, 2 * bins)
 
     @pl.loop(0, n // group)
-    def _(g):
+    def _(step):
+        g = n // group - 1 - step
+
         @pl.loop(0, group)
         def _(i):
             c = g * group + i
@@ -246,9 +277,11 @@
 
         @pl.loop(0, group)
         def _(i):
-            @pl.when(g * group + i > 0)
+            k = g * group + group - 1 - i
+
+            @pl.when(k > 0)
             def _():
-                stack_copy(g * group + i).start()
+                stack_copy(k).start()
 
     own_out = pltpu.make_async_copy(sendb.at[0], out_ref.at[me], own_sem.at[1])
     own_out.start()
@@ -272,26 +305,27 @@
     pairs = rounds * eb * eb
     bins, tables = half_tables(samples)
     group = 4 if n % 4 == 0 else 1
-    flags = available.astype(jnp.bfloat16).reshape(eb, stations, rounds * eb)
-    flags = jnp.pad(flags, ((0, 0), (0, 0), (0, LANES - rounds * eb)))
-    packed = jnp.concatenate([waveforms, flags], axis=-1)
-    wide = samples + LANES
-    packed = packed.reshape(eb, n, local, wide).transpose(1, 0, 2, 3).reshape(n, rows, wide)
+    wide = samples + stations
     bf, f32 = jnp.bfloat16, jnp.float32
     vmem, dma = pltpu.VMEM, pltpu.SemaphoreType.DMA
     anywhere = pl.BlockSpec(memory_space=pl.ANY)
     stacks, scores = pl.pallas_call(
         functools.partial(
-            kernel, n, eb, rounds, local, samples, bins, group,
+            kernel, n, eb, rounds, local, stations, samples, bins, group,
             2.0 / math.sqrt(samples * stations),
         ),
         out_shape=(
             jax.ShapeDtypeStruct((n, rows, samples), bf),
-            jax.ShapeDtypeStruct((pairs, LAGS), f32),
+            jax.ShapeDtypeStruct((rounds, eb, eb, LAGS), f32),
         ),
-        in_specs=[pl.BlockSpec(memory_space=pltpu.SMEM)] + [anywhere] * 5,
+        in_specs=[
+            pl.BlockSpec(memory_space=pltpu.SMEM),
+            pl.BlockSpec(memory_space=pltpu.VMEM),
+        ] + [anywhere] * 5,
         out_specs=(anywhere, pl.BlockSpec(memory_space=pltpu.VMEM)),
         scratch_shapes=[
+            vmem((eb, stations, samples), bf),
+            vmem((n, rows, wide), bf),
             vmem((n, rows, wide), bf),
             vmem(tables[0].shape, bf),
             vmem(tables[1].shape, bf),
@@ -299,7 +333,6 @@
             vmem(tables[3].shape, bf),
             vmem((n * eb, local, 2 * bins), f32),
             vmem((n * rounds * eb, rows, 2 * bins), bf),
-            vmem((n * pairs, local, LAGS), f32),
             vmem((n, pairs, LAGS), f32),
             vmem((n, pairs, LAGS), f32),
             vmem((n, pairs, LAGS), f32),
@@ -312,9 +345,9 @@
         compiler_params=pltpu.CompilerParams(
             collective_id=0, has_side_effects=True, vmem_limit_bytes=56 * 1024 * 1024
         ),
-    )(matching, packed, *(jnp.asarray(t) for t in tables))
+    )(matching, available.transpose(0, 2, 3, 1), waveforms, *(jnp.asarray(t) for t in tables))
     stacks = stacks.reshape(n, eb, local, samples).transpose(1, 0, 2, 3)
-    return stacks.reshape(eb, stations, samples), scores.reshape(rounds, eb, eb, LAGS)
+    return stacks.reshape(eb, stations, samples), scores
 
 
 def plain_body(waveforms, matching, available):
@@ -371,7 +404,11 @@
 
     def body(waveforms, matching, available):
         eb, stations, _ = waveforms.shape
-        if stations % n == 0 and (stations // n) % 8 == 0 and eb * (stations // n) % 16 == 0:
+        local = stations // n
+        pairs = matching.shape[0] * eb * eb
+        if n % 2 == 0 and stations % n == 0 and local % 8 == 0 and 8 <= pairs <= eb * local and (
+            eb * local % 16 == 0 and stations % LANES == 0
+        ):
             return kernel_body(n, waveforms, matching, available)
         return plain_body(waveforms, matching, available)
 

time: 58.5 us -> 52.3 us (0.89)
  the two profiles are of different devices: /device:TPU:0 before, /device:TPU:15 now
where the time goes in v2:
time: 52.3 us; the launch traced here: 52 us
  Pallas kernels  48.2 us (92%)
  local copies, waits for them, and re-layouts  3.14 us (6%)
  between operations  0.64 us (1%)
    pallas_call x1, Pallas kernels, kernel_body(): pl.pallas_call(functools.partial(kernel, n, eb, rounds, local, stations,...  48.2 us
    reshape x1, local copies, waits for them, and re-layouts, kernel_body(): return (stacks.reshape(eb, stations, samples), scores)  1.87 us
    unnamed x1, local copies, waits for them, and re-layouts  1.27 us

profile of v2, /device:TPU:15, one launch (start us, length us, event | category | flops | bytes accessed | tf_op | source)
XLA Modules:
  0.0 52.0 jit_solution(6543309677811467741)
XLA Ops:
  0.6 48.2 %shard_map.86 = (bf16[16,16,1024]{2,1,0:T(8,128)(2,1)}, f32[2,2,2,128]{3,2,1,0:T(2,128)}) custom-call(s32[2,16]{1,0:T(2,128)} %match_ref.1, s32[2,2,2,128]{3,2,1,0:T(2,128)} %bitcast.8, bf16[2,128,1024]{2,1,0:T(8,128)(2,1)} %wave_hbm.1, bf16[1024,1280]{1,0:T(8,128)(2,1)} %constant.8.clone.fwd_hbm, bf16[1280,128]{1,0:T(8,128)(2,1)} %constant.9.clone.ctab_hbm, ...), custom_call_target="tpu_custom_call" | custom-call | tf_op jit(solution)/shard_map/pallas_call | solution.py:312
  48.9 1.9 %copy_bitcast_fusion = bf16[2,128,1024]{2,1,0:T(8,128)(2,1)} fusion(bf16[16,16,1024]{2,1,0:T(8,128)(2,1)} %get-tuple-element.4), kind=kLoop, calls=%fused_computation | loop fusion | bytes 1048576 | tf_op jit(solution)/shard_map/reshape | solution.py:350
  50.8 1.3 %copy.12 = f32[2,2,2,128]{3,2,1,0:T(2,128)} copy(f32[2,2,2,128]{3,2,1,0:T(2,128)} %get-tuple-element.9) | data formatting | bytes 8192

commit v3 on v2

--- a/solution.py
+++ b/solution.py
@@ -211,11 +211,11 @@
 
     @pl.loop(1, n)
     def _(k):
-        part_copy(k).start()
-
-    @pl.loop(1, n)
-    def _(k):
-        part_copy(k).wait_recv()
+        part_copy(n - k).start()
+
+    @pl.loop(1, n)
+    def _(k):
+        part_copy(n - k).wait_recv()
 
     total = part[0]
     for k in range(1, n):
@@ -297,6 +297,18 @@
     own_out.wait()
 
 
+def finish(eb, local, stack_ref, score_ref, out_ref, scores_ref):
+    scores_ref[...] = score_ref[...]
+
+    @pl.loop(0, stack_ref.shape[0] // 2)
+    def _(q):
+        halves = [stack_ref[2 * q + h].astype(jnp.float32) for h in range(2)]
+        for e in range(eb):
+            out_ref[e, pl.ds(pl.multiple_of(q * 2 * local, 2 * local), 2 * local), :] = jnp.concatenate(
+                [half[e * local:(e + 1) * local] for half in halves], axis=0
+            ).astype(jnp.bfloat16)
+
+
 def kernel_body(n, waveforms, matching, available):
     eb, stations, samples = waveforms.shape
     rounds = matching.shape[0]
@@ -304,7 +316,7 @@
     rows = eb * local
     pairs = rounds * eb * eb
     bins, tables = half_tables(samples)
-    group = 4 if n % 4 == 0 else 1
+    group = 8 if n % 8 == 0 else 2
     wide = samples + stations
     bf, f32 = jnp.bfloat16, jnp.float32
     vmem, dma = pltpu.VMEM, pltpu.SemaphoreType.DMA
@@ -346,8 +358,20 @@
             collective_id=0, has_side_effects=True, vmem_limit_bytes=56 * 1024 * 1024
         ),
     )(matching, available.transpose(0, 2, 3, 1), waveforms, *(jnp.asarray(t) for t in tables))
-    stacks = stacks.reshape(n, eb, local, samples).transpose(1, 0, 2, 3)
-    return stacks.reshape(eb, stations, samples), scores
+    steps = 2 if n % 4 == 0 else 1
+    whole = pl.BlockSpec(scores.shape, lambda i: (0, 0, 0, 0))
+    return pl.pallas_call(
+        functools.partial(finish, eb, local),
+        grid=(steps,),
+        out_shape=(
+            jax.ShapeDtypeStruct((eb, stations, samples), bf),
+            jax.ShapeDtypeStruct(scores.shape, f32),
+        ),
+        in_specs=[pl.BlockSpec((n // steps, rows, samples), lambda i: (i, 0, 0)), whole],
+        out_specs=(
+            pl.BlockSpec((eb, stations // steps, samples), lambda i: (0, i, 0)), whole
+        ),
+    )(stacks, scores)
 
 
 def plain_body(waveforms, matching, available):

time: 52.3 us -> 48.8 us (0.933)
  local copies, waits for them, and re-layouts: 3.14 us -> 0 us
    pallas_call x1, Pallas kernels: 48.2 us -> 46.2 us  [kernel_body(): pl.pallas_call(functools.partial(kernel, n, eb, rounds, local, stations,...]
    reshape x1 -> x0, local copies, waits for them, and re-layouts: 1.87 us -> none  [kernel_body(): return (stacks.reshape(eb, stations, samples), scores)]
    pallas_call x0 -> x1, Pallas kernels: none -> 1.78 us  [kernel_body(): pl.pallas_call(functools.partial(finish, eb, local), grid=(steps,), out_s...]
    unnamed x1 -> x0, local copies, waits for them, and re-layouts: 1.27 us -> none
where the time goes in v3:
time: 48.8 us; the launch traced here: 48.7 us
  Pallas kernels  48 us (98%)
  between operations  0.64 us (1%)
    pallas_call x1, Pallas kernels, kernel_body(): pl.pallas_call(functools.partial(kernel, n, eb, rounds, local, stations,...  46.2 us
    pallas_call x1, Pallas kernels, kernel_body(): pl.pallas_call(functools.partial(finish, eb, local), grid=(steps,), out_s...  1.78 us

profile of v3, /device:TPU:15, one launch (start us, length us, event | category | flops | bytes accessed | tf_op | source)
XLA Modules:
  0.0 48.7 jit_solution(14793976605013367902)
XLA Ops:
  0.6 46.2 %shard_map.86 = (bf16[16,16,1024]{2,1,0:T(8,128)(2,1)}, f32[2,2,2,128]{3,2,1,0:T(2,128)}) custom-call(s32[2,16]{1,0:T(2,128)} %match_ref.1, s32[2,2,2,128]{3,2,1,0:T(2,128)} %bitcast.1, bf16[2,128,1024]{2,1,0:T(8,128)(2,1)} %wave_hbm.1, bf16[1024,1280]{1,0:T(8,128)(2,1)} %constant.8.clone.fwd_hbm, bf16[1280,128]{1,0:T(8,128)(2,1)} %constant.9.clone.ctab_hbm, ...), custom_call_target="tpu_custom_call" | custom-call | tf_op jit(solution)/shard_map/pallas_call | solution.py:324
  46.9 1.8 %shard_map.87 = (bf16[2,128,1024]{2,1,0:T(8,128)(2,1)}, f32[2,2,2,128]{3,2,1,0:T(2,128)}) custom-call(bf16[16,16,1024]{2,1,0:T(8,128)(2,1)} %get-tuple-element.4.stack_ref, f32[2,2,2,128]{3,2,1,0:T(2,128)} %get-tuple-element.5.score_ref), custom_call_target="tpu_custom_call" | custom-call | tf_op jit(solution)/shard_map/pallas_call | solution.py:363
